TPU v7x, 256 devices: a whole 4x4x8 slice. The times are simulated.
256 devices in a mesh: row: 16 (over y, z_lo, core), col: 16 (over x, z_hi).
Axes of the slice: x: 4, y: 4, z: 8 (z_hi: 4, z_lo: 2; z = z_hi * 2 + z_lo), core: 2. Of those that a mesh axis runs over, the one named last changes fastest.
Arguments:
- out_grad: float32 [2048, 6144], P('row', 'col'), may hold values from -1.5 to 1.5
- inputs: float32 [2048, 6144], P('row', 'col'), may hold values from -6 to 6
- pre_act: float32 [2048, 12288], P('col', 'row'), may hold values from -6 to 6
- w_in: float32 [6144, 12288], P('col', 'row'), may hold values from -0.078125 to 0.078125
- w_out: float32 [12288, 6144], P('row', 'col'), may hold values from -0.0546875 to 0.0546875
- kept: int32 [8], replicated, may hold values from 64 to 256, as said below
Outputs:
- grad_inputs: float32 [2048, 6144], P('row', 'col')
- grad_w_in: float32 [6144, 12288], P('col', 'row')
- grad_w_out: float32 [12288, 6144], P('row', 'col')
Inputs may be any that keep to these rules, and one draw needn't show every extreme that they name: `kept`: at least one sample keeps all 256 of its rows.
All inputs are finite; a program needn't handle non-finite values.
Results may differ from a plain program's by a relative error of at most 0.00011.
Values sent between devices are 32-bit elements; how exact they have to be, the bound alone decides.
A program may use at most 128 MiB of HBM per device.

v0:
```python
import math

import jax
import jax.numpy as jnp
from jax import lax
from jax.sharding import PartitionSpec as P

PAD = 256


def contract_last(left, right):
    return lax.dot_general(
        left,
        right,
        (((1,), (1,)), ((), ())),
        precision=lax.Precision.HIGHEST,
        preferred_element_type=jnp.float32,
    )


def contract_first(left, right):
    return lax.dot_general(
        left,
        right,
        (((0,), (0,)), ((), ())),
        precision=lax.Precision.HIGHEST,
        preferred_element_type=jnp.float32,
    )


def gelu_pair(pre_values, act_grad):
    normal_cdf = 0.5 * (1.0 + jax.scipy.special.erf(pre_values / math.sqrt(2.0)))
    density = jnp.exp(-0.5 * pre_values * pre_values) / math.sqrt(2.0 * math.pi)
    return (pre_values * normal_cdf, act_grad * (normal_cdf + pre_values * density))


def shards(out_grad, inputs, pre_act, w_in, w_out, kept):
    rows_here = out_grad.shape[0]
    position = lax.axis_index("row") * rows_here + jnp.arange(rows_here, dtype=jnp.int32)
    sample = position // PAD
    matches = sample[:, None] == jnp.arange(kept.shape[0], dtype=jnp.int32)[None, :]
    kept_limit = jnp.sum(jnp.where(matches, kept[None, :], 0), axis=1)
    live_rows = (position % PAD < kept_limit).astype(jnp.float32)
    masked = out_grad * live_rows[:, None]
    grad_all, input_all = (
        lax.all_gather(masked, "row", axis=0, tiled=True),
        lax.all_gather(inputs, "row", axis=0, tiled=True),
    )
    row_block = grad_all
    act_grad = lax.psum_scatter(
        contract_last(row_block, w_out), "col", scatter_dimension=0, tiled=True
    )
    activated, pre_grad = gelu_pair(pre_act, act_grad)
    act_all, pre_grad_all = (
        lax.all_gather(activated, "col", axis=0, tiled=True),
        lax.all_gather(pre_grad, "col", axis=0, tiled=True),
    )
    grad_w_out = contract_first(act_all, grad_all)
    grad_w_in = contract_first(input_all, pre_grad_all)
    row_block = pre_grad_all
    grad_inputs = lax.psum_scatter(
        contract_last(row_block, w_in), "row", scatter_dimension=0, tiled=True
    )
    return (grad_inputs, grad_w_in, grad_w_out)


def solution(mesh):
    return jax.shard_map(
        shards,
        mesh=mesh,
        in_specs=(
            P("row", "col"),
            P("row", "col"),
            P("col", "row"),
            P("col", "row"),
            P("row", "col"),
            P(),
        ),
        out_specs=(P("row", "col"), P("col", "row"), P("row", "col")),
        check_vma=False,
    )
```

profile of v0, /device:TPU:2, one launch (start us, length us, event | category | flops | bytes accessed | tf_op | source)
XLA Modules:
  0.0 490.4 jit_solution(2040387730311528410)
XLA Ops:
  7.2 0.0 copy-start
  7.2 0.0 all-gather.5.cloned.1.call-start
  7.2 0.8 select_reduce_fusion
  8.1 1.7 broadcast_multiply_fusion
  9.8 0.0 all-gather.5.cloned.1.call-update
  9.8 0.0 reduce-scatter.3.cloned.1.call-start
  9.8 41.9 %all-gather.5.cloned.1.call-done = f32[2048,384]{1,0:T(8,128)} async-done(((f32[128,384]{1,0:T(8,128)}), f32[2048,384]{1,0:T(8,128)}) %all-gather.5.cloned.1.call-update) | async-done | bytes 3145744 | tf_op jit(solution)/shard_map/all_gather | solution.py:46
  51.8 0.0 copy-done
  51.8 13.7 %fusion.6 = f32[2048,768]{1,0:T(8,128)} fusion(f32[2048,384]{1,0:T(8,128)} %all-gather.5.cloned.1.call-done, f32[768,384]{1,0:T(8,128)S(1)} %copy-done), kind=kOutput, calls=%fused_computation.19 | convolution fusion | flops 7247757312 | bytes 10616832 | tf_op jit(solution)/shard_map/dot_general | solution.py:12
  65.4 0.0 copy-start.2
  65.4 0.0 copy-start.1
  65.4 0.0 reduce-scatter.3.cloned.1.call-update
  65.4 0.0 all-gather.7.cloned.1.call-start
  65.5 109.2 %reduce-scatter.3.cloned.1.call-done = f32[128,768]{1,0:T(8,128)} async-done(((f32[2048,768]{1,0:T(8,128)}), f32[128,768]{1,0:T(8,128)}) %reduce-scatter.3.cloned.1.call-update) | async-done | bytes 393232 | tf_op jit(solution)/shard_map/reduce_scatter | solution.py:50
  174.7 0.0 copy-done.2
  174.7 2.0 fusion.5
  176.8 0.0 all-gather.7.cloned.1.call-update
  176.8 0.0 all-gather.9.cloned.1.call-start
  176.8 0.5 all-gather.9.cloned.1.call-update
  177.4 0.0 all-gather.11.cloned.1.call-start
  177.4 0.5 all-gather.11.cloned.1.call-update
  178.0 0.2 reduce-scatter.5.cloned.1.call-start
  178.2 96.2 %all-gather.7.cloned.1.call-done = f32[2048,768]{1,0:T(8,128)} async-done(((f32[128,768]{1,0:T(8,128)}), f32[2048,768]{1,0:T(8,128)}) %all-gather.7.cloned.1.call-update) | async-done | bytes 6291472 | tf_op jit(solution)/shard_map/all_gather | solution.py:56
  274.4 0.0 copy-done.1
  274.4 13.1 %fusion.7 = f32[2048,384]{1,0:T(8,128)} fusion(f32[2048,768]{1,0:T(8,128)} %all-gather.7.cloned.1.call-done, f32[384,768]{1,0:T(8,128)S(1)} %copy-done.1), kind=kOutput, calls=%fused_computation.20 | convolution fusion | flops 7247757312 | bytes 10616832 | tf_op jit(solution)/shard_map/dot_general | solution.py:12
  287.5 0.0 reduce-scatter.5.cloned.1.call-update
  287.6 25.3 %all-gather.9.cloned.1.call-done = f32[2048,384]{1,0:T(8,128)} async-done(((f32[128,384]{1,0:T(8,128)}), f32[2048,384]{1,0:T(8,128)}) %all-gather.9.cloned.1.call-update) | async-done | bytes 3145744 | tf_op jit(solution)/shard_map/all_gather | solution.py:47
  312.9 12.5 %convolution_bitcast_fusion = f32[384,768]{0,1:T(8,128)S(1)} fusion(f32[2048,768]{1,0:T(8,128)} %all-gather.7.cloned.1.call-done, f32[2048,384]{1,0:T(8,128)} %all-gather.9.cloned.1.call-done), kind=kOutput, calls=%fused_computation | convolution fusion | flops 7247757312 | bytes 10616832 | tf_op jit(solution)/shard_map/dot_general | solution.py:22
  325.4 1.4 copy.10
  326.8 86.4 %all-gather.11.cloned.1.call-done = f32[2048,768]{1,0:T(8,128)} async-done(((f32[128,768]{1,0:T(8,128)}), f32[2048,768]{1,0:T(8,128)}) %all-gather.11.cloned.1.call-update) | async-done | bytes 6291472 | tf_op jit(solution)/shard_map/all_gather | solution.py:55
  413.1 13.5 %fusion.8 = f32[768,384]{1,0:T(8,128)} fusion(f32[2048,768]{1,0:T(8,128)} %all-gather.11.cloned.1.call-done, f32[2048,384]{1,0:T(8,128)} %all-gather.5.cloned.1.call-done), kind=kOutput, calls=%fused_computation.21 | convolution fusion | flops 7247757312 | bytes 10616832 | tf_op jit(solution)/shard_map/dot_general | solution.py:22
  426.7 56.9 %reduce-scatter.5.cloned.1.call-done = f32[128,384]{1,0:T(8,128)} async-done(((f32[2048,384]{1,0:T(8,128)}), f32[128,384]{1,0:T(8,128)}) %reduce-scatter.5.cloned.1.call-update) | async-done | bytes 196624 | tf_op jit(solution)/shard_map/reduce_scatter | solution.py:61
  (2 shorter events, 0.0 us)
Async XLA Ops:
  7.2 44.6 %copy-start = (f32[768,384]{1,0:T(8,128)S(1)}, f32[768,384]{1,0:T(8,128)}, u32[]{:S(2)}) copy-start(f32[768,384]{1,0:T(8,128)} %param.10) | copy-start | bytes 3538948
  7.2 44.6 %all-gather.5.cloned.1.call-start = ((), (), s32[]{:S(2)}) async-start(), calls=%async_computation.2 | async-start | bytes 3342336 | tf_op jit(solution)/shard_map/all_gather | solution.py:46
  9.8 164.9 %reduce-scatter.3.cloned.1.call-start = ((), (), s32[]{:S(2)}) async-start(), calls=%async_computation.3 | async-start | bytes 6684672 | tf_op jit(solution)/shard_map/reduce_scatter | solution.py:50
  65.4 109.3 %copy-start.2 = (f32[128,768]{1,0:T(8,128)S(1)}, f32[128,768]{1,0:T(8,128)}, u32[]{:S(2)}) copy-start(f32[128,768]{1,0:T(8,128)} %param.8) | copy-start | bytes 1179652
  65.4 209.0 %copy-start.1 = (f32[384,768]{1,0:T(8,128)S(1)}, f32[384,768]{1,0:T(8,128)}, u32[]{:S(2)}) copy-start(f32[384,768]{1,0:T(8,128)} %param.9) | copy-start | bytes 3538948
  65.4 208.9 %all-gather.7.cloned.1.call-start = ((), (), s32[]{:S(2)}) async-start(), calls=%async_computation.4 | async-start | bytes 6684672 | tf_op jit(solution)/shard_map/all_gather | solution.py:56
  176.8 136.1 %all-gather.9.cloned.1.call-start = ((), (), s32[]{:S(2)}) async-start(), calls=%async_computation.6 | async-start | bytes 3342336 | tf_op jit(solution)/shard_map/all_gather | solution.py:47
  177.4 235.8 %all-gather.11.cloned.1.call-start = ((), (), s32[]{:S(2)}) async-start(), calls=%async_computation.7 | async-start | bytes 6684672 | tf_op jit(solution)/shard_map/all_gather | solution.py:55
  178.0 305.6 %reduce-scatter.5.cloned.1.call-start = ((), (), s32[]{:S(2)}) async-start(), calls=%async_computation.5 | async-start | bytes 3342336 | tf_op jit(solution)/shard_map/reduce_scatter | solution.py:61
Sparse Core Ops, SparseCore 0:
  10.4 41.2 all-gather.4
  65.6 109.1 reduce-scatter.2
  177.8 96.5 all-gather.6
  276.1 36.7 all-gather.8
  315.8 97.3 all-gather.10
  416.1 67.4 reduce-scatter.4
where the time goes:
time: 491 us; the launch traced here: 490 us
  waiting for transfers between devices  417 us (85%)
  matrix products  52.8 us (11%)
  between operations  14.1 us (3%)
    reduce_scatter x1, waiting for transfers between devices, shards(): lax.psum_scatter(contract_last(row_block, w_out), 'col', scatter_dimensio...  109 us
    all_gather x1, waiting for transfers between devices, shards(): lax.all_gather(pre_grad, 'col', axis=0, tiled=True)  96.2 us
    all_gather x1, waiting for transfers between devices, shards(): lax.all_gather(activated, 'col', axis=0, tiled=True)  86.4 us
    reduce_scatter x1, waiting for transfers between devices, shards(): lax.psum_scatter(contract_last(row_block, w_in), 'row', scatter_dimension...  56.9 us
    all_gather x1, waiting for transfers between devices, shards(): lax.all_gather(masked, 'row', axis=0, tiled=True)  41.9 us
    dot_general x2, matrix products, contract_last(): lax.dot_general(left, right, (((1,), (1,)), ((), ())), precision=lax.Prec...  26.8 us
    dot_general x2, matrix products, contract_first(): lax.dot_general(left, right, (((0,), (0,)), ((), ())), precision=lax.Prec...  26 us
    all_gather x1, waiting for transfers between devices, shards(): lax.all_gather(inputs, 'row', axis=0, tiled=True)  25.3 us
  transfers between devices with their start and end apart: 6, of which 6 were waited for; matrix products, arithmetic and copies ran while one was open for 8% of the time, Pallas kernels for 0%

commit v1 on v0

v1 whole, which is shorter than its diff:
```python
import functools
import math

import jax
import jax.numpy as jnp
from jax import lax
from jax.experimental import pallas as pl
from jax.experimental.pallas import tpu as pltpu
from jax.sharding import PartitionSpec as P

PAD = 256
SAMPLES = 8
TOKENS = 2048
TILE = 8
SAMPLE_TILES = PAD // TILE
TILES = TOKENS // TILE
ROWS = 128
OWN = ROWS // TILE
D = 384
F = 768
LC = 256
J = F // LC
COPIES = 160
MESH = pl.DeviceIdType.MESH
F32 = jnp.float32
BF16 = jnp.bfloat16


def split(value):
    high = value.astype(BF16)
    return high, (value - high.astype(F32)).astype(BF16)


def product(left, right, dims):
    def one(a, b):
        return lax.dot_general(a, b, (dims, ((), ())), preferred_element_type=F32)

    (lh, ll), (rh, rl) = left, right
    return one(lh, rh) + (one(ll, rh) + one(lh, rl))


NT = ((1,), (1,))
NN = ((1,), (0,))


def normal_cdf(value):
    return 0.5 * (1.0 + lax.erf(value * (1.0 / math.sqrt(2.0))))


def density(value):
    return jnp.exp(-0.5 * value * value) * (1.0 / math.sqrt(2.0 * math.pi))


def kernel(
    tb,
    kept_ref, g_ref, x_ref, p_ref, win_hbm, wout_hbm,
    dx_ref, dwin_ref, dwout_ref,
    src, inv,
    g_all, x_all, p_all, part, rx1, rx2, rz1, rz2, pg,
    gp_hi, gp_lo, gt_hi, gt_lo, xt_hi, xt_lo,
    win_f, wout_f, win_hi, win_lo, wout_hi, wout_lo,
    dxp, dxs, dsib, dy1, dy2, dz, dwt, stage, rows_buf,
    send_sem, recv_sem, local_sem,
):
    bp = tb // 16
    half = bp // 2
    steps = tb // PAD
    row, col = lax.axis_index("row"), lax.axis_index("col")
    y, zl, core = row // 4, (row // 2) % 2, row % 2
    x, zh = col // 4, col % 4

    def at_row(yy, ll, cc):
        return {"row": (yy % 4) * 4 + ll * 2 + cc, "col": col}

    def at_col(xx, hh):
        return {"row": row, "col": (xx % 4) * 4 + hh % 4}

    xp, xm = at_col(x + 1, zh), at_col(x + 3, zh)
    zp, zm = at_col(x, zh + 1), at_col(x, zh + 3)
    yp, ym = at_row(y + 1, zl, core), at_row(y + 3, zl, core)
    zlp, sib = at_row(y, 1 - zl, core), at_row(y, zl, 1 - core)
    peers = (xp, xm, zp, zm, yp, ym, zlp, sib)

    barrier = pltpu.get_barrier_semaphore()
    for peer in peers:
        pl.semaphore_signal(barrier, inc=1, device_id=peer, device_id_type=MESH)

    weights = [
        pltpu.make_async_copy(wout_hbm, wout_f, local_sem.at[0]),
        pltpu.make_async_copy(win_hbm, win_f, local_sem.at[1]),
    ]
    for w in weights:
        w.start()

    started = []

    def send(source, target, peer):
        k = len(started)
        copy = pltpu.make_async_remote_copy(
            src_ref=source, dst_ref=target, send_sem=send_sem.at[k], recv_sem=recv_sem.at[k],
            device_id=peer, device_id_type=MESH,
        )
        copy.start()
        started.append(copy)
        return copy

    limit = kept_ref[row // 2] - (row % 2) * ROWS
    position = lax.broadcasted_iota(jnp.int32, (OWN, TILE, D), 0) * TILE + lax.broadcasted_iota(
        jnp.int32, (OWN, TILE, D), 1
    )
    g_all[pl.ds(row * OWN, OWN)] = jnp.where(position < limit, g_ref[...], 0.0)
    x_all[pl.ds(row * OWN, OWN)] = x_ref[...]
    p_all[pl.ds(col * OWN, OWN)] = p_ref[...]

    pl.semaphore_wait(barrier, len(peers))

    def row_gather(ref):
        def block(yy, ll, cc):
            return ref.at[pl.ds(((yy % 4) * 4 + ll * 2 + cc) * OWN, OWN)]

        def move(peer, *where):
            return send(block(*where), block(*where), peer)

        own = (y, zl, core)
        c = {"z": move(zlp, *own), "up": move(yp, *own), "down": move(ym, *own)}
        s = [move(sib, *own)]
        yield
        c["z"].wait_recv()
        other = (y, 1 - zl, core)
        c["up2"], c["down2"] = move(yp, *other), move(ym, *other)
        s.append(move(sib, *other))
        yield
        c["up"].wait_recv()
        c["far"] = move(yp, y + 3, zl, core)
        s.append(move(sib, y + 3, zl, core))
        c["down"].wait_recv()
        s.append(move(sib, y + 1, zl, core))
        yield
        c["down2"].wait_recv()
        c["far2"] = move(ym, y + 1, 1 - zl, core)
        s.append(move(sib, y + 1, 1 - zl, core))
        c["up2"].wait_recv()
        s.append(move(sib, y + 3, 1 - zl, core))
        yield
        c["far"].wait_recv()
        s.append(move(sib, y + 2, zl, core))
        c["far2"].wait_recv()
        s.append(move(sib, y + 2, 1 - zl, core))
        yield
        for copy in s:
            copy.wait_recv()
        yield

    def col_gather(block, size):
        lo, hi = (0, size // 2), (size // 2, size // 2)

        def move(peer, xx, hh, span=(0, size)):
            ref = block(xx % 4, hh % 4, *span)
            return send(ref, ref, peer)

        c = {}
        c["za"], c["zb"] = move(zp, x, zh), move(zm, x, zh)
        c["p0"], c["m0"] = move(xp, x, zh), move(xm, x, zh)
        yield
        c["za"].wait_recv()
        c["zc"] = move(zp, x, zh + 3, lo)
        c["p3"], c["m3"] = move(xp, x, zh + 3), move(xm, x, zh + 3)
        c["zb"].wait_recv()
        c["zd"] = move(zm, x, zh + 1, hi)
        c["p1"], c["m1"] = move(xp, x, zh + 1), move(xm, x, zh + 1)
        yield
        c["zc"].wait_recv()
        c["zd"].wait_recv()
        c["p2"], c["m2"] = move(xp, x, zh + 2), move(xm, x, zh + 2)
        yield
        c["p0"].wait_recv()
        c["f0"] = move(xp, x + 3, zh)
        c["m3"].wait_recv()
        c["f3"] = move(xm, x + 1, zh + 3)
        yield
        c["p1"].wait_recv()
        c["f1"] = move(xp, x + 3, zh + 1)
        c["m2"].wait_recv()
        c["f2"] = move(xm, x + 1, zh + 2)
        yield
        for name in ("m0", "m1", "p3", "p2", "f0", "f3", "f1", "f2"):
            c[name].wait_recv()
        yield

    def col_sum(j):
        def blocks(xx, first=0, count=4):
            return part.at[j, pl.ds((xx % 4) * 4 + first, count)]

        def piece(hh, start=0, count=bp):
            return part.at[j, x * 4 + hh % 4, pl.ds(start, count)]

        c = {}

        def partial(xx):
            base = pl.multiple_of((xx % 4) * (4 * bp), 4 * bp)
            span = pl.ds(base, 4 * bp)
            units = pl.ds(j * LC, LC)
            value = product(
                (gp_hi[span], gp_lo[span]), (wout_hi[units], wout_lo[units]), NT
            )
            part[j, pl.ds((xx % 4) * 4, 4)] = value.reshape(4, bp, LC)

        partial(x + 2)
        c["a"] = send(blocks(x + 2, 0, 2), rx1.at[j, 0], xp)
        c["b"] = send(blocks(x + 2, 2, 2), rx1.at[j, 1], xm)
        yield
        partial(x + 1)
        c["c"] = send(blocks(x + 1, 2, 2), rx2.at[j, 0, pl.ds(2, 2)], xp)
        partial(x + 3)
        c["d"] = send(blocks(x + 3, 0, 2), rx2.at[j, 1, pl.ds(0, 2)], xm)
        yield
        partial(x)
        yield
        c["a"].wait_recv()
        part[j, pl.ds(((x + 1) % 4) * 4, 2)] += rx1[j, 0]
        c["e"] = send(blocks(x + 1, 0, 2), rx2.at[j, 0, pl.ds(0, 2)], xp)
        c["b"].wait_recv()
        part[j, pl.ds(((x + 3) % 4) * 4 + 2, 2)] += rx1[j, 1]
        c["f"] = send(blocks(x + 3, 2, 2), rx2.at[j, 1, pl.ds(2, 2)], xm)
        yield
        for name in ("c", "d", "e", "f"):
            c[name].wait_recv()
        part[j, pl.ds(x * 4, 4)] += rx2[j, 0] + rx2[j, 1]
        c["g"] = send(piece(zh + 2, 0, half), rz1.at[j, 0], zp)
        c["h"] = send(piece(zh + 2, half, half), rz1.at[j, 1], zm)
        c["i"] = send(piece(zh + 1, half, half), rz2.at[j, 0, pl.ds(half, half)], zp)
        c["k"] = send(piece(zh + 3, 0, half), rz2.at[j, 1, pl.ds(0, half)], zm)
        yield
        c["g"].wait_recv()
        part[j, x * 4 + (zh + 1) % 4, pl.ds(0, half)] += rz1[j, 0]
        c["l"] = send(piece(zh + 1, 0, half), rz2.at[j, 0, pl.ds(0, half)], zp)
        c["h"].wait_recv()
        part[j, x * 4 + (zh + 3) % 4, pl.ds(half, half)] += rz1[j, 1]
        c["m"] = send(piece(zh + 3, half, half), rz2.at[j, 1, pl.ds(half, half)], zm)
        yield
        for name in ("i", "k", "l", "m"):
            c[name].wait_recv()
        total = part[j, x * 4 + zh] + rz2[j, 0] + rz2[j, 1]
        mine = rows_buf[:, pl.ds(j * LC, LC)]
        slope = normal_cdf(mine) + mine * density(mine)
        pg[j, pl.ds(pl.multiple_of(col * bp, bp), bp)] = total * slope
        yield

    def pg_block(j):
        def block(xx, hh, start, count):
            first = pl.multiple_of((xx * 4 + hh) * bp + start, TILE)
            return pg.at[j, pl.ds(first, count)]

        return block

    def p_block(xx, hh, start, count):
        return p_all.at[pl.ds((xx * 4 + hh) * OWN + start, count)]

    def tables():
        live = [(kept_ref[s] + (TILE - 1)) // TILE for s in range(SAMPLES)]
        ends = []
        for s in range(SAMPLES):
            ends.append(live[s] + (ends[-1] if ends else 0))

        def fill(i, carry):
            source = i
            for s in range(SAMPLES):
                source = source + jnp.where(i >= ends[s], SAMPLE_TILES - live[s], 0)
            src[i] = jnp.where(i < ends[-1], source, -1)
            return carry

        lax.fori_loop(0, tb // TILE, fill, 0)
        for s in range(SAMPLES):
            begin = ends[s] - live[s]

            def place(i, carry, s=s, begin=begin):
                inv[s * SAMPLE_TILES + i] = jnp.where(i < live[s], begin + i, -1)
                return carry

            lax.fori_loop(0, SAMPLE_TILES, place, 0)

    def fetch(ref, first, count, masked):
        width = ref.shape[-1]

        def one(i, carry):
            at = src[first + i]
            tile = ref[jnp.maximum(at, 0)]
            if masked:
                tile = jnp.where(at >= 0, tile, 0.0)
            stage[pl.ds(pl.multiple_of(i * TILE, TILE), TILE), pl.ds(0, width)] = tile
            return carry

        lax.fori_loop(0, count, one, 0, unroll=4)
        return stage[pl.ds(0, count * TILE), pl.ds(0, width)]

    def pack_g():
        def body(t, carry):
            value = fetch(g_all, t * SAMPLE_TILES, SAMPLE_TILES, True)
            span = pl.ds(pl.multiple_of(t * PAD, PAD), PAD)
            gp_hi[span], gp_lo[span] = split(value)
            return carry

        lax.fori_loop(0, steps, body, 0)

    def transposed(ref, to_hi, to_lo, masked):
        def body(t, carry):
            value = fetch(ref, t * SAMPLE_TILES, SAMPLE_TILES, masked).T
            high, low = split(value)
            to_hi[t] = high
            to_lo[t] = low
            return carry

        lax.fori_loop(0, steps, body, 0)

    def own_rows():
        def one(i, carry):
            at = src[col * (bp // TILE) + i]
            rows_buf[pl.ds(pl.multiple_of(i * TILE, TILE), TILE)] = p_all[jnp.maximum(at, 0)]
            return carry

        lax.fori_loop(0, bp // TILE, one, 0)

    def w_out_grad():
        dwt[...] = jnp.zeros_like(dwt)

        def body(t, carry):
            value = fetch(p_all, t * SAMPLE_TILES, SAMPLE_TILES, False)
            act = split(value * normal_cdf(value))
            dwt[...] += product((gt_hi[t], gt_lo[t]), act, NN)
            return carry

        lax.fori_loop(0, steps, body, 0)
        dwout_ref[...] = dwt[...].T

    def w_in_grad(j):
        units = pl.ds(j * LC, LC)

        def body(t, carry):
            value = split(pg[j, pl.ds(pl.multiple_of(t * PAD, PAD), PAD)])
            dwin_ref[:, units] += product((xt_hi[t], xt_lo[t]), value, NN)
            return carry

        lax.fori_loop(0, steps, body, 0)

    def x_grad(j):
        def body(t, carry):
            value = split(pg[j, pl.ds(pl.multiple_of(t * PAD, PAD), PAD)])
            out = product(value, (win_hi[j], win_lo[j]), NT).reshape(SAMPLE_TILES, TILE, D)
            span = pl.ds(t * SAMPLE_TILES, SAMPLE_TILES)
            if j == 0:
                dxp[span] = out
            else:
                dxp[span] += out
            return carry

        lax.fori_loop(0, steps, body, 0)

    def row_sum():
        def spread(yy, cc):
            yy = yy % 4

            def one(i, carry):
                ll = i // OWN
                at = inv[(yy * 4 + ll * 2 + cc) * OWN + i % OWN]
                tile = dxp[jnp.maximum(at, 0)]
                dxs[cc, yy, i] = jnp.where(at >= 0, tile, 0.0)
                return carry

            lax.fori_loop(0, 2 * OWN, one, 0, unroll=4)

        order = (y + 2, y + 1, y + 3, y)
        s = []
        for k, yy in enumerate(order):
            spread(yy, 1 - core)
            s.append(send(dxs.at[1 - core, yy % 4], dsib.at[k], sib))
        yield
        for yy in order:
            spread(yy, core)

        def blocks(yy, ll):
            return dxs.at[core, yy % 4, pl.ds(ll * OWN, OWN)]

        def add_sib(k):
            s[k].wait_recv()
            dxs[core, order[k] % 4] += dsib[k]

        c = {}
        add_sib(0)
        c["a"] = send(blocks(y + 2, 0), dy1.at[0], yp)
        c["b"] = send(blocks(y + 2, 1), dy1.at[1], ym)
        add_sib(1)
        c["c"] = send(blocks(y + 1, 1), dy2.at[0, pl.ds(OWN, OWN)], yp)
        add_sib(2)
        c["d"] = send(blocks(y + 3, 0), dy2.at[1, pl.ds(0, OWN)], ym)
        add_sib(3)
        yield
        c["a"].wait_recv()
        dxs[core, (y + 1) % 4, pl.ds(0, OWN)] += dy1[0]
        c["e"] = send(blocks(y + 1, 0), dy2.at[0, pl.ds(0, OWN)], yp)
        c["b"].wait_recv()
        dxs[core, (y + 3) % 4, pl.ds(OWN, OWN)] += dy1[1]
        c["f"] = send(blocks(y + 3, 1), dy2.at[1, pl.ds(OWN, OWN)], ym)
        yield
        for name in ("c", "d", "e", "f"):
            c[name].wait_recv()
        dxs[core, y] += dy2[0] + dy2[1]
        c["z"] = send(blocks(y, 1 - zl), dz, zlp)
        yield
        c["z"].wait_recv()
        dx_ref[...] = dxs[core, y, pl.ds(zl * OWN, OWN)] + dz[...]
        yield

    g_steps, x_steps = row_gather(g_all), row_gather(x_all)
    p_steps = col_gather(p_block, OWN)
    sums = [col_sum(j) for j in range(J)]
    gathers = [col_gather(pg_block(j), bp) for j in range(J)]

    def go(steps_of, count=1):
        for _ in range(count):
            next(steps_of)

    go(g_steps)
    go(p_steps)
    tables()
    weights[0].wait()
    wout_hi[...], wout_lo[...] = split(wout_f[...])
    go(g_steps, 2)
    go(p_steps)
    go(g_steps, 3)
    pack_g()
    go(sums[0], 2)
    go(p_steps)
    go(x_steps)
    go(sums[0])
    go(sums[1], 3)
    go(sums[2], 3)
    weights[1].wait()
    for j in range(J):
        win_hi[j], win_lo[j] = split(win_f[:, pl.ds(j * LC, LC)])
    go(x_steps, 2)
    go(p_steps, 2)
    go(x_steps, 3)
    transposed(g_all, gt_hi, gt_lo, True)
    dwin_ref[...] = jnp.zeros_like(dwin_ref)
    go(sums[0])
    go(sums[1])
    go(p_steps)
    own_rows()
    go(sums[0])
    go(sums[2])
    go(sums[0])
    go(sums[1])
    go(sums[0])
    go(gathers[0])
    go(sums[1])
    go(sums[2])
    go(sums[1])
    go(gathers[1])
    go(gathers[0])
    transposed(x_all, xt_hi, xt_lo, False)
    go(sums[2])
    go(gathers[0])
    go(sums[2])
    go(gathers[2])
    go(gathers[1])
    go(gathers[0], 2)
    go(gathers[1])
    go(gathers[2])
    w_out_grad()
    go(gathers[0])
    x_grad(0)
    go(gathers[2])
    go(gathers[1], 2)
    w_in_grad(0)
    go(gathers[1])
    x_grad(1)
    go(gathers[2], 2)
    w_in_grad(1)
    go(gathers[2])
    x_grad(2)
    tail = row_sum()
    go(tail, 4)
    w_in_grad(2)
    go(tail)
    for copy in started:
        copy.wait_send()
    assert len(started) <= COPIES


def grad_kernel(tb, out_grad, inputs, pre_act, w_in, w_out, kept):
    bp = tb // 16
    vmem = pl.BlockSpec(memory_space=pltpu.VMEM)
    anywhere = pl.BlockSpec(memory_space=pl.ANY)

    def room(*shape, dtype=F32):
        return pltpu.VMEM(shape, dtype)

    half = functools.partial(room, dtype=BF16)
    steps = tb // PAD
    dx, dwin, dwout = pl.pallas_call(
        functools.partial(kernel, tb),
        out_shape=(
            jax.ShapeDtypeStruct((OWN, TILE, D), F32),
            jax.ShapeDtypeStruct((D, F), F32),
            jax.ShapeDtypeStruct((F, D), F32),
        ),
        in_specs=[pl.BlockSpec(memory_space=pltpu.SMEM), vmem, vmem, vmem, anywhere, anywhere],
        out_specs=(vmem, vmem, vmem),
        scratch_shapes=[
            pltpu.SMEM((tb // TILE,), jnp.int32),
            pltpu.SMEM((TILES,), jnp.int32),
            room(TILES, TILE, D),
            room(TILES, TILE, D),
            room(TILES, TILE, F),
            room(J, 16, bp, LC),
            room(J, 2, 2, bp, LC),
            room(J, 2, 4, bp, LC),
            room(J, 2, bp // 2, LC),
            room(J, 2, bp, LC),
            room(J, tb, LC),
            half(tb, D),
            half(tb, D),
            half(steps, D, PAD),
            half(steps, D, PAD),
            half(steps, D, PAD),
            half(steps, D, PAD),
            room(D, F),
            room(F, D),
            half(J, D, LC),
            half(J, D, LC),
            half(F, D),
            half(F, D),
            room(tb // TILE, TILE, D),
            room(2, 4, 2 * OWN, TILE, D),
            room(4, 2 * OWN, TILE, D),
            room(2, OWN, TILE, D),
            room(2, 2 * OWN, TILE, D),
            room(OWN, TILE, D),
            room(D, F),
            room(PAD, F),
            room(bp, F),
            pltpu.SemaphoreType.DMA((COPIES,)),
            pltpu.SemaphoreType.DMA((COPIES,)),
            pltpu.SemaphoreType.DMA((2,)),
        ],
        compiler_params=pltpu.CompilerParams(
            collective_id=tb // PAD, has_side_effects=True, vmem_limit_bytes=64 * 1024 * 1024
        ),
        cost_estimate=pl.CostEstimate(flops=12 * tb * D * F * 2, bytes_accessed=6 * 1024 * 1024, transcendentals=0),
    )(
        kept,
        out_grad.reshape(OWN, TILE, D),
        inputs.reshape(OWN, TILE, D),
        pre_act.reshape(OWN, TILE, F),
        w_in,
        w_out,
    )
    return dx.reshape(ROWS, D), dwin, dwout


def shards(*args):
    return grad_kernel(TOKENS, *args)


def solution(mesh):
    return jax.shard_map(
        shards,
        mesh=mesh,
        in_specs=(
            P("row", "col"),
            P("row", "col"),
            P("col", "row"),
            P("col", "row"),
            P("row", "col"),
            P(),
        ),
        out_specs=(P("row", "col"), P("col", "row"), P("row", "col")),
        check_vma=False,
    )
```

time: 491 us -> 238 us (0.48)
  waiting for transfers between devices: 417 us -> 0 us
  Pallas kernels: 0 us -> 230 us
  matrix products: 52.8 us -> 0 us
  between operations: 14.1 us -> 0.64 us
    all_gather x4 -> x0, waiting for transfers between devices: 250 us -> none  [the longest x1 96.2 us: shards(): lax.all_gather(pre_grad, 'col', axis=0, tiled=True)]
    pallas_call x0 -> x1, Pallas kernels: none -> 230 us  [grad_kernel(): pl.pallas_call(functools.partial(kernel, tb), out_shape=(jax.ShapeDtypeSt...]
    reduce_scatter x2 -> x0, waiting for transfers between devices: 166 us -> none  [the longest x1 109 us: shards(): lax.psum_scatter(contract_last(row_block, w_out), 'col', scatter_dimensio...]
    dot_general x4 -> x0, matrix products: 52.8 us -> none  [the longest x2 26.8 us: contract_last(): lax.dot_general(left, right, (((1,), (1,)), ((), ())), precision=lax.Prec...]
  transfers between devices with their start and end apart: 6 -> 0, of which waited for: 6 -> 0; matrix products, arithmetic and copies ran while one was open for 8% -> 0% of each run, Pallas kernels for 0% -> 0%
where the time goes in v1:
time: 238 us; the launch traced here: 236 us
  Pallas kernels  230 us (97%)
  local copies, waits for them, and re-layouts  5.09 us (2%)
    pallas_call x1, Pallas kernels, grad_kernel(): pl.pallas_call(functools.partial(kernel, tb), out_shape=(jax.ShapeDtypeSt...  230 us
    unnamed x5, local copies, waits for them, and re-layouts  5.09 us

profile of v1, /device:TPU:2, one launch (start us, length us, event | category | flops | bytes accessed | tf_op | source)
XLA Modules:
  0.0 235.6 jit_solution(2946616183657560791)
XLA Ops:
  0.6 229.9 %shard_map.85 = (f32[16,8,384]{2,1,0:T(8,128)}, f32[384,768]{1,0:T(8,128)}, f32[768,384]{1,0:T(8,128)}) custom-call(s32[8]{0:T(128)} %kept_ref.1, f32[16,8,384]{2,1,0:T(8,128)} %bitcast.6, f32[16,8,384]{2,1,0:T(8,128)} %bitcast.7, f32[16,8,768]{2,1,0:T(8,128)} %bitcast.5, f32[384,768]{1,0:T(8,128)} %win_hbm.1, f32[768,384]{1,0:T(8,128)} %wout_hbm.1), custom_call_target="tpu_custom_call" | custom-call | flops 14495514624 | bytes 6291456 | tf_op jit(solution)/shard_map/pallas_call | solution.py:500
  230.5 1.6 copy.12
  232.1 0.0 copy-start
  232.1 2.5 %copy.13 = f32[384,768]{1,0:T(8,128)} copy(f32[384,768]{1,0:T(8,128)} %get-tuple-element.13) | data formatting | bytes 2359296
  234.6 0.0 copy-done
  234.6 1.0 copy.14
Async XLA Ops:
  232.1 2.5 %copy-start = (f32[768,384]{1,0:T(8,128)S(1)}, f32[768,384]{1,0:T(8,128)}, u32[]{:S(2)}) copy-start(f32[768,384]{1,0:T(8,128)} %get-tuple-element.14) | copy-start | bytes 3538948

commit v2 on v1

--- a/solution.py
+++ b/solution.py
@@ -20,7 +20,19 @@
 F = 768
 LC = 256
 J = F // LC
-COPIES = 160
+COPIES = 176
+CROSS = 8
+BUCKETS = (1280, 1536, 2048)
+ORDER = (
+    "g", "p", "tab", "wo", "q", "x", "g", "g", "g", "p", "p", "p", "x", "x", "x", "g", "g", "q", "g", "q", "q",
+    "x", "p", "g", "p", "p", "x", "q", "g", "pack", "s0", "s0", "s0", "s0", "s1", "s1", "s1", "s1", "s2", "s2",
+    "s2", "s2", "p", "q", "x", "x", "wi", "s0", "s0", "gt", "x", "gt", "xt", "xt", "s1", "s1", "q", "q", "s2",
+    "s2", "p", "q", "own", "dwo", "s0", "dwo", "s1", "dwo", "s0", "s0", "s2", "dwo", "s1", "s1", "dwo", "s0",
+    "a0", "s2", "s2", "a0", "s1", "a1", "a0", "a0", "a1", "s2", "a2", "a1", "a1", "a0", "a0", "a0", "a2", "a2",
+    "a2", "a0", "a1", "a1", "a1", "a2", "a2", "a0", "dx0", "dx0", "dx0", "a1", "a2", "dx0", "dw0", "dw0", "a2",
+    "a1", "dx1", "dx1", "dx1", "a2", "dx1", "dx2", "dx2", "dx2", "dx2", "t", "t", "dw1", "t", "dw1", "t", "dw2",
+    "t", "dw2", "t", "t", "t", "t", "t",
+)
 MESH = pl.DeviceIdType.MESH
 F32 = jnp.float32
 BF16 = jnp.bfloat16
@@ -63,7 +75,8 @@
     send_sem, recv_sem, local_sem,
 ):
     bp = tb // 16
-    half = bp // 2
+    half = bp // 16 * 8
+    rest = bp - half
     steps = tb // PAD
     row, col = lax.axis_index("row"), lax.axis_index("col")
     y, zl, core = row // 4, (row // 2) % 2, row % 2
@@ -133,17 +146,20 @@
         c["up"].wait_recv()
         c["far"] = move(yp, y + 3, zl, core)
         s.append(move(sib, y + 3, zl, core))
+        yield
         c["down"].wait_recv()
         s.append(move(sib, y + 1, zl, core))
         yield
         c["down2"].wait_recv()
         c["far2"] = move(ym, y + 1, 1 - zl, core)
         s.append(move(sib, y + 1, 1 - zl, core))
+        yield
         c["up2"].wait_recv()
         s.append(move(sib, y + 3, 1 - zl, core))
         yield
         c["far"].wait_recv()
         s.append(move(sib, y + 2, zl, core))
+        yield
         c["far2"].wait_recv()
         s.append(move(sib, y + 2, 1 - zl, core))
         yield
@@ -151,37 +167,43 @@
             copy.wait_recv()
         yield
 
-    def col_gather(block, size):
-        lo, hi = (0, size // 2), (size // 2, size // 2)
-
-        def move(peer, xx, hh, span=(0, size)):
+    def col_gather(block, size, z_first=True):
+        cut = size // 2 if size < 16 else size // 16 * TILE
+        lo, hi = (0, cut), (cut, size - cut)
+        u, v, ups, vps = (zh, x, (zp, zm), (xp, xm)) if z_first else (x, zh, (xp, xm), (zp, zm))
+
+        def move(peer, uu, vv, span=(0, size)):
+            xx, hh = (vv, uu) if z_first else (uu, vv)
             ref = block(xx % 4, hh % 4, *span)
             return send(ref, ref, peer)
 
         c = {}
-        c["za"], c["zb"] = move(zp, x, zh), move(zm, x, zh)
-        c["p0"], c["m0"] = move(xp, x, zh), move(xm, x, zh)
-        yield
-        c["za"].wait_recv()
-        c["zc"] = move(zp, x, zh + 3, lo)
-        c["p3"], c["m3"] = move(xp, x, zh + 3), move(xm, x, zh + 3)
-        c["zb"].wait_recv()
-        c["zd"] = move(zm, x, zh + 1, hi)
-        c["p1"], c["m1"] = move(xp, x, zh + 1), move(xm, x, zh + 1)
-        yield
-        c["zc"].wait_recv()
-        c["zd"].wait_recv()
-        c["p2"], c["m2"] = move(xp, x, zh + 2), move(xm, x, zh + 2)
+        c["ua"], c["ub"] = move(ups[0], u, v), move(ups[1], u, v)
+        c["p0"], c["m0"] = move(vps[0], u, v), move(vps[1], u, v)
         yield
         c["p0"].wait_recv()
-        c["f0"] = move(xp, x + 3, zh)
+        c["f0"] = move(vps[0], u, v + 3)
+        yield
+        c["ua"].wait_recv()
+        c["uc"] = move(ups[0], u + 3, v, lo)
+        c["p3"], c["m3"] = move(vps[0], u + 3, v), move(vps[1], u + 3, v)
+        yield
+        c["ub"].wait_recv()
+        c["ud"] = move(ups[1], u + 1, v, hi)
+        c["p1"], c["m1"] = move(vps[0], u + 1, v), move(vps[1], u + 1, v)
+        yield
+        c["uc"].wait_recv()
+        c["ud"].wait_recv()
+        c["p2"], c["m2"] = move(vps[0], u + 2, v), move(vps[1], u + 2, v)
+        yield
         c["m3"].wait_recv()
-        c["f3"] = move(xm, x + 1, zh + 3)
+        c["f3"] = move(vps[1], u + 3, v + 1)
         yield
         c["p1"].wait_recv()
-        c["f1"] = move(xp, x + 3, zh + 1)
+        c["f1"] = move(vps[0], u + 1, v + 3)
+        yield
         c["m2"].wait_recv()
-        c["f2"] = move(xm, x + 1, zh + 2)
+        c["f2"] = move(vps[1], u + 2, v + 1)
         yield
         for name in ("m0", "m1", "p3", "p2", "f0", "f3", "f1", "f2"):
             c[name].wait_recv()
@@ -211,6 +233,7 @@
         yield
         partial(x + 1)
         c["c"] = send(blocks(x + 1, 2, 2), rx2.at[j, 0, pl.ds(2, 2)], xp)
+        yield
         partial(x + 3)
         c["d"] = send(blocks(x + 3, 0, 2), rx2.at[j, 1, pl.ds(0, 2)], xm)
         yield
@@ -219,6 +242,7 @@
         c["a"].wait_recv()
         part[j, pl.ds(((x + 1) % 4) * 4, 2)] += rx1[j, 0]
         c["e"] = send(blocks(x + 1, 0, 2), rx2.at[j, 0, pl.ds(0, 2)], xp)
+        yield
         c["b"].wait_recv()
         part[j, pl.ds(((x + 3) % 4) * 4 + 2, 2)] += rx1[j, 1]
         c["f"] = send(blocks(x + 3, 2, 2), rx2.at[j, 1, pl.ds(2, 2)], xm)
@@ -226,17 +250,18 @@
         for name in ("c", "d", "e", "f"):
             c[name].wait_recv()
         part[j, pl.ds(x * 4, 4)] += rx2[j, 0] + rx2[j, 1]
-        c["g"] = send(piece(zh + 2, 0, half), rz1.at[j, 0], zp)
-        c["h"] = send(piece(zh + 2, half, half), rz1.at[j, 1], zm)
-        c["i"] = send(piece(zh + 1, half, half), rz2.at[j, 0, pl.ds(half, half)], zp)
+        c["g"] = send(piece(zh + 2, 0, half), rz1.at[j, 0, pl.ds(0, half)], zp)
+        c["h"] = send(piece(zh + 2, half, rest), rz1.at[j, 1, pl.ds(0, rest)], zm)
+        c["i"] = send(piece(zh + 1, half, rest), rz2.at[j, 0, pl.ds(half, rest)], zp)
         c["k"] = send(piece(zh + 3, 0, half), rz2.at[j, 1, pl.ds(0, half)], zm)
         yield
         c["g"].wait_recv()
-        part[j, x * 4 + (zh + 1) % 4, pl.ds(0, half)] += rz1[j, 0]
+        part[j, x * 4 + (zh + 1) % 4, pl.ds(0, half)] += rz1[j, 0, pl.ds(0, half)]
         c["l"] = send(piece(zh + 1, 0, half), rz2.at[j, 0, pl.ds(0, half)], zp)
+        yield
         c["h"].wait_recv()
-        part[j, x * 4 + (zh + 3) % 4, pl.ds(half, half)] += rz1[j, 1]
-        c["m"] = send(piece(zh + 3, half, half), rz2.at[j, 1, pl.ds(half, half)], zm)
+        part[j, x * 4 + (zh + 3) % 4, pl.ds(half, rest)] += rz1[j, 1, pl.ds(0, rest)]
+        c["m"] = send(piece(zh + 3, half, rest), rz2.at[j, 1, pl.ds(half, rest)], zm)
         yield
         for name in ("i", "k", "l", "m"):
             c[name].wait_recv()
@@ -253,8 +278,16 @@
 
         return block
 
-    def p_block(xx, hh, start, count):
-        return p_all.at[pl.ds((xx * 4 + hh) * OWN + start, count)]
+    def p_block(offset):
+        def block(xx, hh, start, count):
+            return p_all.at[pl.ds((xx * 4 + hh) * OWN + offset + start, count)]
+
+        return block
+
+    def quarters(body, parts):
+        for k in range(parts):
+            lax.fori_loop(k * steps // parts, (k + 1) * steps // parts, body, 0)
+            yield
 
     def tables():
         live = [(kept_ref[s] + (TILE - 1)) // TILE for s in range(SAMPLES)]
@@ -278,6 +311,7 @@
                 return carry
 
             lax.fori_loop(0, SAMPLE_TILES, place, 0)
+        yield
 
     def fetch(ref, first, count, masked):
         width = ref.shape[-1]
@@ -300,7 +334,7 @@
             gp_hi[span], gp_lo[span] = split(value)
             return carry
 
-        lax.fori_loop(0, steps, body, 0)
+        yield from quarters(body, 1)
 
     def transposed(ref, to_hi, to_lo, masked):
         def body(t, carry):
@@ -310,7 +344,7 @@
             to_lo[t] = low
             return carry
 
-        lax.fori_loop(0, steps, body, 0)
+        yield from quarters(body, 2)
 
     def own_rows():
         def one(i, carry):
@@ -319,6 +353,18 @@
             return carry
 
         lax.fori_loop(0, bp // TILE, one, 0)
+        yield
+
+    def w_out_split():
+        weights[0].wait()
+        wout_hi[...], wout_lo[...] = split(wout_f[...])
+        yield
+
+    def w_in_split():
+        weights[1].wait()
+        for j in range(J):
+            win_hi[j], win_lo[j] = split(win_f[:, pl.ds(j * LC, LC)])
+        yield
 
     def w_out_grad():
         dwt[...] = jnp.zeros_like(dwt)
@@ -329,8 +375,9 @@
             dwt[...] += product((gt_hi[t], gt_lo[t]), act, NN)
             return carry
 
-        lax.fori_loop(0, steps, body, 0)
+        yield from quarters(body, 4)
         dwout_ref[...] = dwt[...].T
+        yield
 
     def w_in_grad(j):
         units = pl.ds(j * LC, LC)
@@ -340,7 +387,8 @@
             dwin_ref[:, units] += product((xt_hi[t], xt_lo[t]), value, NN)
             return carry
 
-        lax.fori_loop(0, steps, body, 0)
+        dwin_ref[:, units] = jnp.zeros((D, LC), F32)
+        yield from quarters(body, 2)
 
     def x_grad(j):
         def body(t, carry):
@@ -353,7 +401,7 @@
                 dxp[span] += out
             return carry
 
-        lax.fori_loop(0, steps, body, 0)
+        yield from quarters(body, 4)
 
     def row_sum():
         def spread(yy, cc):
@@ -384,19 +432,24 @@
             s[k].wait_recv()
             dxs[core, order[k] % 4] += dsib[k]
 
+        yield
         c = {}
         add_sib(0)
         c["a"] = send(blocks(y + 2, 0), dy1.at[0], yp)
         c["b"] = send(blocks(y + 2, 1), dy1.at[1], ym)
+        yield
         add_sib(1)
         c["c"] = send(blocks(y + 1, 1), dy2.at[0, pl.ds(OWN, OWN)], yp)
+        yield
         add_sib(2)
         c["d"] = send(blocks(y + 3, 0), dy2.at[1, pl.ds(0, OWN)], ym)
+        yield
         add_sib(3)
         yield
         c["a"].wait_recv()
         dxs[core, (y + 1) % 4, pl.ds(0, OWN)] += dy1[0]
         c["e"] = send(blocks(y + 1, 0), dy2.at[0, pl.ds(0, OWN)], yp)
+        yield
         c["b"].wait_recv()
         dxs[core, (y + 3) % 4, pl.ds(OWN, OWN)] += dy1[1]
         c["f"] = send(blocks(y + 3, 1), dy2.at[1, pl.ds(OWN, OWN)], ym)
@@ -410,78 +463,30 @@
         dx_ref[...] = dxs[core, y, pl.ds(zl * OWN, OWN)] + dz[...]
         yield
 
-    g_steps, x_steps = row_gather(g_all), row_gather(x_all)
-    p_steps = col_gather(p_block, OWN)
-    sums = [col_sum(j) for j in range(J)]
-    gathers = [col_gather(pg_block(j), bp) for j in range(J)]
-
-    def go(steps_of, count=1):
-        for _ in range(count):
-            next(steps_of)
-
-    go(g_steps)
-    go(p_steps)
-    tables()
-    weights[0].wait()
-    wout_hi[...], wout_lo[...] = split(wout_f[...])
-    go(g_steps, 2)
-    go(p_steps)
-    go(g_steps, 3)
-    pack_g()
-    go(sums[0], 2)
-    go(p_steps)
-    go(x_steps)
-    go(sums[0])
-    go(sums[1], 3)
-    go(sums[2], 3)
-    weights[1].wait()
+    parts = {
+        "g": row_gather(g_all),
+        "x": row_gather(x_all),
+        "p": col_gather(p_block(0), OWN - CROSS),
+        "q": col_gather(p_block(OWN - CROSS), CROSS, z_first=False),
+        "tab": tables(),
+        "wo": w_out_split(),
+        "wi": w_in_split(),
+        "pack": pack_g(),
+        "own": own_rows(),
+        "gt": transposed(g_all, gt_hi, gt_lo, True),
+        "xt": transposed(x_all, xt_hi, xt_lo, False),
+        "dwo": w_out_grad(),
+        "t": row_sum(),
+    }
     for j in range(J):
-        win_hi[j], win_lo[j] = split(win_f[:, pl.ds(j * LC, LC)])
-    go(x_steps, 2)
-    go(p_steps, 2)
-    go(x_steps, 3)
-    transposed(g_all, gt_hi, gt_lo, True)
-    dwin_ref[...] = jnp.zeros_like(dwin_ref)
-    go(sums[0])
-    go(sums[1])
-    go(p_steps)
-    own_rows()
-    go(sums[0])
-    go(sums[2])
-    go(sums[0])
-    go(sums[1])
-    go(sums[0])
-    go(gathers[0])
-    go(sums[1])
-    go(sums[2])
-    go(sums[1])
-    go(gathers[1])
-    go(gathers[0])
-    transposed(x_all, xt_hi, xt_lo, False)
-    go(sums[2])
-    go(gathers[0])
-    go(sums[2])
-    go(gathers[2])
-    go(gathers[1])
-    go(gathers[0], 2)
-    go(gathers[1])
-    go(gathers[2])
-    w_out_grad()
-    go(gathers[0])
-    x_grad(0)
-    go(gathers[2])
-    go(gathers[1], 2)
-    w_in_grad(0)
-    go(gathers[1])
-    x_grad(1)
-    go(gathers[2], 2)
-    w_in_grad(1)
-    go(gathers[2])
-    x_grad(2)
-    tail = row_sum()
-    go(tail, 4)
-    w_in_grad(2)
-    go(tail)
+        parts[f"s{j}"] = col_sum(j)
+        parts[f"a{j}"] = col_gather(pg_block(j), bp)
+        parts[f"dx{j}"] = x_grad(j)
+        parts[f"dw{j}"] = w_in_grad(j)
+    for name in ORDER:
+        next(parts[name])
+    for part_left in parts.values():
+        assert next(part_left, None) is None
     for copy in started:
         copy.wait_send()
     assert len(started) <= COPIES
@@ -515,7 +520,7 @@
             room(J, 16, bp, LC),
             room(J, 2, 2, bp, LC),
             room(J, 2, 4, bp, LC),
-            room(J, 2, bp // 2, LC),
+            room(J, 2, bp - bp // 16 * 8, LC),
             room(J, 2, bp, LC),
             room(J, tb, LC),
             half(tb, D),
@@ -559,7 +564,9 @@
 
 
 def shards(*args):
-    return grad_kernel(TOKENS, *args)
+    tiles = jnp.sum((args[-1] + (TILE - 1)) // TILE)
+    index = sum((tiles > rows // TILE).astype(jnp.int32) for rows in BUCKETS[:-1])
+    return lax.switch(index, [functools.partial(grad_kernel, rows) for rows in BUCKETS], *args)
 
 
 def solution(mesh):

time: 238 us -> 177 us (0.74)
  Pallas kernels: 230 us -> 167 us
    pallas_call x1, Pallas kernels: 230 us -> 167 us  [grad_kernel(): pl.pallas_call(functools.partial(kernel, tb), out_shape=(jax.ShapeDtypeSt...]
where the time goes in v2:
time: 177 us; the launch traced here: 176 us
  Pallas kernels  167 us (94%)
  local copies, waits for them, and re-layouts  5.09 us (3%)
  between operations  1.94 us (1%)
    pallas_call x1, Pallas kernels, grad_kernel(): pl.pallas_call(functools.partial(kernel, tb), out_shape=(jax.ShapeDtypeSt...  167 us
    unnamed x5, local copies, waits for them, and re-layouts  5.09 us

profile of v2, /device:TPU:2, one launch (start us, length us, event | category | flops | bytes accessed | tf_op | source)
XLA Modules:
  0.0 176.0 jit_solution(17287886669407248399)
XLA Ops:
  0.6 1.3 fusion
  3.2 167.7 %conditional.1 = (f32[384,768]{1,0:T(8,128)}, f32[768,384]{1,0:T(8,128)}, f32[128,384]{1,0:T(8,128)}) conditional(s32[]{:T(128)} %clamp.3, (f32[128,384]{1,0:T(8,128)}, f32[128,384]{1,0:T(8,128)}, f32[128,768]{1,0:T(8,128)}, s32[8]{0:T(128)}, f32[384,768]{1,0:T(8,128)}, /*index=5*/f32[768,384]{1,0:T(8,128)}) %tuple.19, ...), branch_computations={%region_1.2_spmd, %region_2.3_spmd, %region_3.4_spmd} | conditional | flops 14495514624 | bytes 6291480 | solution.py:569
  3.2 167.2 %branch_0_fun.1 = (f32[16,8,384]{2,1,0:T(8,128)}, f32[384,768]{1,0:T(8,128)}, f32[768,384]{1,0:T(8,128)}) custom-call(s32[8]{0:T(128)} %get-tuple-element.36.kept_ref, f32[16,8,384]{2,1,0:T(8,128)} %bitcast.18, f32[16,8,384]{2,1,0:T(8,128)} %bitcast.21, f32[16,8,768]{2,1,0:T(8,128)} %bitcast.15, f32[384,768]{1,0:T(8,128)} %get-tuple-element.40.win_hbm, ...), custom_call_target="tpu_custom_call" | custom-call | flops 9059696640 | bytes 6291456 | tf_op jit(solution)/shard_map/cond/branch_0_fun/pallas_call | solution.py:505
  170.9 1.6 copy.24
  172.6 0.0 copy-start
  172.6 2.5 %copy.25 = f32[384,768]{1,0:T(8,128)} copy(f32[384,768]{1,0:T(8,128)} %get-tuple-element.80) | data formatting | bytes 2359296
  175.0 0.0 copy-done
  175.0 1.0 copy.26
Async XLA Ops:
  172.6 2.5 %copy-start = (f32[768,384]{1,0:T(8,128)S(1)}, f32[768,384]{1,0:T(8,128)}, u32[]{:S(2)}) copy-start(f32[768,384]{1,0:T(8,128)} %get-tuple-element.81) | copy-start | bytes 3538948

commit v3 on v2

v3 whole, which is shorter than its diff:
```python
import functools
import math

import jax
import jax.numpy as jnp
from jax import lax
from jax.experimental import pallas as pl
from jax.experimental.pallas import tpu as pltpu
from jax.sharding import PartitionSpec as P

PAD = 256
SAMPLES = 8
TOKENS = 2048
TILE = 8
SAMPLE_TILES = PAD // TILE
TILES = TOKENS // TILE
ROWS = 128
OWN = ROWS // TILE
D = 384
F = 768
COPIES = 192
HALVES = 16
ORDER = (
    "g", "o", "tab", "tab", "tab", "tab", "o", "wo", "q", "g", "g", "g", "o", "o", "p", "g", "g", "q", "q", "q",
    "g", "o", "o", "o", "p", "g", "q", "g", "pack", "o", "s0", "wi", "p", "p", "o", "own", "q", "s0", "s0", "s1",
    "gt", "gt", "q", "q", "s0", "s1", "s1", "s2", "p", "p", "p", "q", "s1", "s0", "s0", "s2", "s2", "s1", "s1",
    "s0", "a0", "p", "s1", "a1", "s2", "a0", "a0", "a0", "p", "a1", "a1", "a1", "x", "s2", "s2", "dwo", "a0",
    "a0", "dwo", "s2", "a0", "a2", "a1", "a1", "dwo", "a0", "a1", "dwf", "a1", "a2", "a2", "a2", "x", "x", "x",
    "a0", "dx0", "a2", "a1", "dx1", "a2", "t0", "t0", "a2", "x", "x", "t0", "x", "a2", "t0", "t0", "t0", "t0",
    "a2", "dx2", "t1", "t1", "t0", "x", "t1", "t1", "t1", "t1", "x", "xt", "t1", "t0", "t1", "xt", "dw0", "t0",
    "t1", "dw1", "dw2", "t1",
)
PLANS = {10: ((4, 4, 2), 5), 12: ((4, 4, 4), 6), 16: ((6, 6, 4), 8)}
LC = 256
LANES = F // LC
MESH = pl.DeviceIdType.MESH
F32 = jnp.float32
BF16 = jnp.bfloat16


def split(value):
    high = value.astype(BF16)
    return high, (value - high.astype(F32)).astype(BF16)


def product(left, right):
    def one(a, b):
        return jnp.dot(a, b, preferred_element_type=F32)

    (lh, ll), (rh, rl) = left, right
    return one(lh, rh) + (one(ll, rh) + one(lh, rl))


def normal_cdf(value):
    return 0.5 * (1.0 + lax.erf(value * (1.0 / math.sqrt(2.0))))


def density(value):
    return jnp.exp(-0.5 * value * value) * (1.0 / math.sqrt(2.0 * math.pi))


def cumulative(values):
    ends, total = [], 0
    for value in values:
        total = total + value
        ends.append(total)
    return ends


def kernel(
    slots, chunks, cross,
    kept_ref, g_ref, x_ref, p_ref, win_hbm, wout_hbm,
    dx_ref, dwin_ref, dwout_ref,
    src, inv,
    g_all, x_all, p_main, p_over, part, rx1, rx2, rz1, rz2, pg,
    gp_hi, gp_lo, gt_hi, gt_lo, xt_hi, xt_lo,
    win_f, wout_f, win_hi, win_lo, wout_hi, wout_lo,
    dxp, dxs, dsib, dy1, dy2, dz, dwt, acc, stage, mine, counts,
    send_sem, recv_sem, local_sem,
):
    spare = OWN - slots
    first_slot = [end - t for end, t in zip(cumulative(chunks), chunks)]
    row, col = lax.axis_index("row"), lax.axis_index("col")
    y, zl, core = row // 4, (row // 2) % 2, row % 2
    x, zh = col // 4, col % 4

    def at_row(yy, ll, cc):
        return {"row": (yy % 4) * 4 + ll * 2 + cc, "col": col}

    def at_col(xx, hh):
        return {"row": row, "col": (xx % 4) * 4 + hh % 4}

    xp, xm = at_col(x + 1, zh), at_col(x + 3, zh)
    zp, zm = at_col(x, zh + 1), at_col(x, zh + 3)
    yp, ym = at_row(y + 1, zl, core), at_row(y + 3, zl, core)
    zlp, sib = at_row(y, 1 - zl, core), at_row(y, zl, 1 - core)
    peers = (xp, xm, zp, zm, yp, ym, zlp, sib)

    barrier = pltpu.get_barrier_semaphore()
    for peer in peers:
        pl.semaphore_signal(barrier, inc=1, device_id=peer, device_id_type=MESH)

    weights = [
        pltpu.make_async_copy(wout_hbm, wout_f, local_sem.at[0]),
        pltpu.make_async_copy(win_hbm, win_f, local_sem.at[1]),
    ]
    for w in weights:
        w.start()

    started = []

    def send(source, target, peer):
        k = len(started)
        copy = pltpu.make_async_remote_copy(
            src_ref=source, dst_ref=target, send_sem=send_sem.at[k], recv_sem=recv_sem.at[k],
            device_id=peer, device_id_type=MESH,
        )
        copy.start()
        started.append(copy)
        return copy

    limit = kept_ref[row // 2] - (row % 2) * ROWS
    position = lax.broadcasted_iota(jnp.int32, (OWN, TILE, D), 0) * TILE + lax.broadcasted_iota(
        jnp.int32, (OWN, TILE, D), 1
    )
    g_all[pl.ds(row * OWN, OWN)] = jnp.where(position < limit, g_ref[...], 0.0)
    x_all[pl.ds(row * OWN, OWN)] = x_ref[...]
    p_main[pl.ds(col * slots, slots)] = p_ref[pl.ds(0, slots)]
    if spare:
        p_over[pl.ds(col * spare, spare)] = p_ref[pl.ds(slots, spare)]

    pl.semaphore_wait(barrier, len(peers))

    def lanes(n):
        return pl.ds(pl.multiple_of(n * LC, LC), LC)

    def row_gather(ref):
        def block(yy, ll, cc):
            return ref.at[pl.ds(((yy % 4) * 4 + ll * 2 + cc) * OWN, OWN)]

        def move(peer, *where):
            return send(block(*where), block(*where), peer)

        own = (y, zl, core)
        c = {"z": move(zlp, *own), "up": move(yp, *own), "down": move(ym, *own)}
        s = [move(sib, *own)]
        yield
        c["z"].wait_recv()
        other = (y, 1 - zl, core)
        c["up2"], c["down2"] = move(yp, *other), move(ym, *other)
        s.append(move(sib, *other))
        yield
        c["up"].wait_recv()
        c["far"] = move(yp, y + 3, zl, core)
        s.append(move(sib, y + 3, zl, core))
        yield
        c["down"].wait_recv()
        s.append(move(sib, y + 1, zl, core))
        yield
        c["down2"].wait_recv()
        c["far2"] = move(ym, y + 1, 1 - zl, core)
        s.append(move(sib, y + 1, 1 - zl, core))
        yield
        c["up2"].wait_recv()
        s.append(move(sib, y + 3, 1 - zl, core))
        yield
        c["far"].wait_recv()
        s.append(move(sib, y + 2, zl, core))
        yield
        c["far2"].wait_recv()
        s.append(move(sib, y + 2, 1 - zl, core))
        yield
        for copy in s:
            copy.wait_recv()
        yield

    def col_gather(block, size, z_first=True):
        cut = size // 2 if size < 16 else size // 16 * TILE
        lo, hi = (0, cut), (cut, size - cut)
        u, v, ups, vps = (zh, x, (zp, zm), (xp, xm)) if z_first else (x, zh, (xp, xm), (zp, zm))

        def move(peer, uu, vv, span=(0, size)):
            xx, hh = (vv, uu) if z_first else (uu, vv)
            ref = block(xx % 4, hh % 4, *span)
            return send(ref, ref, peer)

        c = {}
        c["ua"], c["ub"] = move(ups[0], u, v), move(ups[1], u, v)
        c["p0"], c["m0"] = move(vps[0], u, v), move(vps[1], u, v)
        yield
        c["p0"].wait_recv()
        c["f0"] = move(vps[0], u, v + 3)
        yield
        c["ua"].wait_recv()
        c["uc"] = move(ups[0], u + 3, v, lo)
        c["p3"], c["m3"] = move(vps[0], u + 3, v), move(vps[1], u + 3, v)
        yield
        c["ub"].wait_recv()
        c["ud"] = move(ups[1], u + 1, v, hi)
        c["p1"], c["m1"] = move(vps[0], u + 1, v), move(vps[1], u + 1, v)
        yield
        c["uc"].wait_recv()
        c["ud"].wait_recv()
        c["p2"], c["m2"] = move(vps[0], u + 2, v), move(vps[1], u + 2, v)
        yield
        c["m3"].wait_recv()
        c["f3"] = move(vps[1], u + 3, v + 1)
        yield
        c["p1"].wait_recv()
        c["f1"] = move(vps[0], u + 1, v + 3)
        yield
        c["m2"].wait_recv()
        c["f2"] = move(vps[1], u + 2, v + 1)
        yield
        for name in ("m0", "m1", "p3", "p2", "f0", "f3", "f1", "f2"):
            c[name].wait_recv()
        yield

    def col_sum(j):
        bp = chunks[j] * TILE
        half = bp // 16 * TILE
        rest = bp - half

        def blocks(xx, first=0, count=4):
            return part[j].at[pl.ds((xx % 4) * 4 + first, count)]

        def piece(hh, start, count):
            return part[j].at[x * 4 + hh % 4, pl.ds(start, count)]

        c = {}

        span = pl.ds(HALVES * TILE * first_slot[j], HALVES * bp)
        left = gp_hi[span], gp_lo[span]

        def body(n, carry):
            value = product(left, (wout_hi[n], wout_lo[n])).reshape(HALVES, bp, LC)
            part[j][:, :, lanes(n)] = value
            return carry

        lax.fori_loop(0, LANES, body, 0)
        c["a"] = send(blocks(x + 2, 0, 2), rx1[j].at[0], xp)
        c["b"] = send(blocks(x + 2, 2, 2), rx1[j].at[1], xm)
        c["c"] = send(blocks(x + 1, 2, 2), rx2[j].at[0, pl.ds(2, 2)], xp)
        c["d"] = send(blocks(x + 3, 0, 2), rx2[j].at[1, pl.ds(0, 2)], xm)
        yield
        c["a"].wait_recv()
        part[j][pl.ds(((x + 1) % 4) * 4, 2)] += rx1[j][0]
        c["e"] = send(blocks(x + 1, 0, 2), rx2[j].at[0, pl.ds(0, 2)], xp)
        yield
        c["b"].wait_recv()
        part[j][pl.ds(((x + 3) % 4) * 4 + 2, 2)] += rx1[j][1]
        c["f"] = send(blocks(x + 3, 2, 2), rx2[j].at[1, pl.ds(2, 2)], xm)
        yield
        for name in ("c", "d", "e", "f"):
            c[name].wait_recv()
        part[j][pl.ds(x * 4, 4)] += rx2[j][0] + rx2[j][1]
        c["g"] = send(piece(zh + 2, 0, half), rz1[j].at[0, pl.ds(0, half)], zp)
        c["h"] = send(piece(zh + 2, half, rest), rz1[j].at[1, pl.ds(0, rest)], zm)
        c["i"] = send(piece(zh + 1, half, rest), rz2[j].at[0, pl.ds(half, rest)], zp)
        c["k"] = send(piece(zh + 3, 0, half), rz2[j].at[1, pl.ds(0, half)], zm)
        yield
        c["g"].wait_recv()
        part[j][x * 4 + (zh + 1) % 4, pl.ds(0, half)] += rz1[j][0, pl.ds(0, half)]
        c["l"] = send(piece(zh + 1, 0, half), rz2[j].at[0, pl.ds(0, half)], zp)
        yield
        c["h"].wait_recv()
        part[j][x * 4 + (zh + 3) % 4, pl.ds(half, rest)] += rz1[j][1, pl.ds(0, rest)]
        c["m"] = send(piece(zh + 3, half, rest), rz2[j].at[1, pl.ds(half, rest)], zm)
        yield
        for name in ("i", "k", "l", "m"):
            c[name].wait_recv()
        total = part[j][x * 4 + zh] + rz2[j][0] + rz2[j][1]
        rows = mine[j][...]
        slope = normal_cdf(rows) + rows * density(rows)
        pg[j][pl.ds(pl.multiple_of(col * bp, bp), bp)] = total * slope
        yield

    def pg_block(j):
        bp = chunks[j] * TILE

        def block(xx, hh, start, count):
            first = pl.multiple_of((xx * 4 + hh) * bp + start, TILE)
            return pg[j].at[pl.ds(first, count)]

        return block

    def p_block(ref, per_block, offset):
        def block(xx, hh, start, count):
            return ref.at[pl.ds((xx * 4 + hh) * per_block + offset + start, count)]

        return block

    def tables():
        live = [
            jnp.clip((kept_ref[b // 2] + (TILE - 1)) // TILE - b % 2 * OWN, 0, OWN)
            for b in range(HALVES)
        ]
        kept_here = [jnp.minimum(n, slots) for n in live]
        over = [n - k for n, k in zip(live, kept_here)]
        over_end = cumulative(over)
        free_end = cumulative([slots - k for k in kept_here])
        for b in range(HALVES):
            counts[0, b] = live[b]
            counts[1, b] = kept_here[b]
            counts[2, b] = over_end[b] - over[b]
            counts[3, b] = free_end[b] - slots
        yield

        def fill_block(b, carry):
            here, free = counts[1, b], counts[3, b]
            for j, t in enumerate(chunks):

                def fill(i, carry, j=j, t=t):
                    k = first_slot[j] + i
                    at = -1
                    if spare:
                        e = free + k
                        moved = e + slots
                        for n in range(HALVES - 1):
                            moved = moved + jnp.where(e >= over_end[n], OWN - over[n], 0)
                        at = jnp.where(e < over_end[-1], moved, -1)
                    src[HALVES * first_slot[j] + b * t + i] = jnp.where(k < here, b * OWN + k, at)
                    return carry

                lax.fori_loop(0, t, fill, 0)
            return carry

        lax.fori_loop(0, HALVES // 2, fill_block, 0)
        yield
        lax.fori_loop(HALVES // 2, HALVES, fill_block, 0)
        yield

        def place_block(b, carry):
            here = counts[0, b]

            def stay(k, carry):
                inv[b * OWN + k] = jnp.where(k < here, b * slots + k, -1)
                return carry

            lax.fori_loop(0, slots, stay, 0)
            if spare:
                begin = counts[2, b]

                def leave(i, carry):
                    e = begin + i
                    slot = e + kept_here[0]
                    for n in range(HALVES - 1):
                        slot = slot + jnp.where(e >= free_end[n], kept_here[n + 1], 0)
                    inv[b * OWN + slots + i] = jnp.where(slots + i < here, slot, -1)
                    return carry

                lax.fori_loop(0, spare, leave, 0)
            return carry

        lax.fori_loop(0, HALVES, place_block, 0)
        yield

    strips = slots // 2

    def fetch(ref, strip, masked):
        width = ref.shape[-1]

        def one(i, carry):
            at = src[strip * SAMPLE_TILES + i]
            tile = ref[jnp.maximum(at, 0)]
            if masked:
                tile = jnp.where(at >= 0, tile, 0.0)
            stage[pl.ds(pl.multiple_of(i * TILE, TILE), TILE), pl.ds(0, width)] = tile
            return carry

        lax.fori_loop(0, SAMPLE_TILES, one, 0, unroll=4)
        return stage[:, pl.ds(0, width)]

    def moved_tile(at, tile):
        if not spare:
            return tile
        at = jnp.maximum(at, 0)
        place = at % OWN - slots
        index = at // OWN * spare + jnp.maximum(place, 0)
        return jnp.where(place >= 0, p_over[index], tile)

    def fetch_p(strip, j):
        def one(i, carry):
            n = (strip - first_slot[j] // 2) * SAMPLE_TILES + i
            own = p_main[n // chunks[j] * slots + first_slot[j] + n % chunks[j]]
            at = src[strip * SAMPLE_TILES + i]
            stage[pl.ds(pl.multiple_of(i * TILE, TILE), TILE)] = moved_tile(at, own)
            return carry

        lax.fori_loop(0, SAMPLE_TILES, one, 0, unroll=4)

    def own_rows():
        for j, t in enumerate(chunks):

            def one(i, carry, j=j, t=t):
                at = src[HALVES * first_slot[j] + col * t + i]
                mine[j][pl.ds(pl.multiple_of(i * TILE, TILE), TILE)] = moved_tile(
                    at, p_ref[first_slot[j] + i]
                )
                return carry

            lax.fori_loop(0, t, one, 0)
        yield

    def pack_g():
        def body(strip, carry):
            span = pl.ds(pl.multiple_of(strip * PAD, PAD), PAD)
            gp_hi[span], gp_lo[span] = split(fetch(g_all, strip, True))
            return carry

        lax.fori_loop(0, strips, body, 0)
        yield

    def transposed(ref, to_hi, to_lo, masked):
        def body(strip, carry):
            high, low = split(fetch(ref, strip, masked).T)
            to_hi[strip] = high
            to_lo[strip] = low
            return carry

        lax.fori_loop(0, strips // 2, body, 0)
        yield
        lax.fori_loop(strips // 2, strips, body, 0)
        yield

    def w_out_split():
        weights[0].wait()

        def body(n, carry):
            rows = pl.ds(pl.multiple_of(n * LC, LC), LC)
            wout_hi[n], wout_lo[n] = split(wout_f[rows].T)
            return carry

        lax.fori_loop(0, LANES, body, 0)
        yield

    def w_in_split():
        weights[1].wait()

        def body(n, carry):
            win_hi[n], win_lo[n] = split(win_f[:, lanes(n)].T)
            return carry

        lax.fori_loop(0, LANES, body, 0)
        yield

    def w_out_grad():
        dwt[...] = jnp.zeros_like(dwt)
        for j, t in enumerate(chunks):

            def body(strip, carry, j=j):
                fetch_p(strip, j)
                left = gt_hi[strip], gt_lo[strip]

                def step(n, carry):
                    value = stage[:, lanes(n)]
                    dwt[n] += product(left, split(value * normal_cdf(value)))
                    return carry

                return lax.fori_loop(0, LANES, step, carry)

            lax.fori_loop(first_slot[j] // 2, (first_slot[j] + t) // 2, body, 0)
            yield

    def w_out_last():
        def body(n, carry):
            dwout_ref[pl.ds(pl.multiple_of(n * LC, LC), LC)] = dwt[n].T
            return carry

        lax.fori_loop(0, LANES, body, 0)
        yield

    def w_in_grad(j):
        if j == 0:
            dwin_ref[...] = jnp.zeros_like(dwin_ref)

        def body(i, carry):
            strip = first_slot[j] // 2 + i
            span = pl.ds(pl.multiple_of(i * PAD, PAD), PAD)
            left = xt_hi[strip], xt_lo[strip]

            def step(n, carry):
                dwin_ref[:, lanes(n)] += product(left, split(pg[j][span, lanes(n)]))
                return carry

            return lax.fori_loop(0, LANES, step, carry)

        lax.fori_loop(0, chunks[j] // 2, body, 0)
        yield

    def x_grad(j):
        t = chunks[j]

        def body(i, carry):
            span = pl.ds(pl.multiple_of(i * PAD, PAD), PAD)
            acc[...] = jnp.zeros_like(acc)

            def step(n, carry):
                left = split(pg[j][span, lanes(n)])
                acc[...] += product(left, (win_hi[n], win_lo[n])).reshape(acc.shape)
                return carry

            lax.fori_loop(0, LANES, step, carry)

            def place(q, carry):
                tile = i * SAMPLE_TILES + q
                dxp[tile // t * slots + first_slot[j] + tile % t] = acc[q]
                return carry

            return lax.fori_loop(0, SAMPLE_TILES, place, carry, unroll=4)

        lax.fori_loop(0, t // 2, body, 0)
        yield

    def row_sum(n, low, high):
        size = high - low

        def spread(yy, cc):
            yy = yy % 4

            def one(i, carry):
                ll, k = i // size, i % size
                at = inv[(yy * 4 + ll * 2 + cc) * OWN + low + k]
                tile = dxp[jnp.maximum(at, 0)]
                dxs[n][cc, yy, i] = jnp.where(at >= 0, tile, 0.0)
                return carry

            lax.fori_loop(0, 2 * size, one, 0, unroll=2)

        order = (y + 2, y + 1, y + 3, y)
        s = []
        for k, yy in enumerate(order):
            spread(yy, 1 - core)
            s.append(send(dxs[n].at[1 - core, yy % 4], dsib[n].at[k], sib))
        yield
        for yy in order:
            spread(yy, core)

        def blocks(yy, ll):
            return dxs[n].at[core, yy % 4, pl.ds(ll * size, size)]

        def add_sib(k):
            s[k].wait_recv()
            dxs[n][core, order[k] % 4] += dsib[n][k]

        yield
        c = {}
        add_sib(0)
        c["a"] = send(blocks(y + 2, 0), dy1[n].at[0], yp)
        c["b"] = send(blocks(y + 2, 1), dy1[n].at[1], ym)
        yield
        add_sib(1)
        c["c"] = send(blocks(y + 1, 1), dy2[n].at[0, pl.ds(size, size)], yp)
        yield
        add_sib(2)
        c["d"] = send(blocks(y + 3, 0), dy2[n].at[1, pl.ds(0, size)], ym)
        yield
        add_sib(3)
        yield
        c["a"].wait_recv()
        dxs[n][core, (y + 1) % 4, pl.ds(0, size)] += dy1[n][0]
        c["e"] = send(blocks(y + 1, 0), dy2[n].at[0, pl.ds(0, size)], yp)
        yield
        c["b"].wait_recv()
        dxs[n][core, (y + 3) % 4, pl.ds(size, size)] += dy1[n][1]
        c["f"] = send(blocks(y + 3, 1), dy2[n].at[1, pl.ds(size, size)], ym)
        yield
        for name in ("c", "d", "e", "f"):
            c[name].wait_recv()
        dxs[n][core, y] += dy2[n][0] + dy2[n][1]
        c["z"] = send(blocks(y, 1 - zl), dz[n], zlp)
        yield
        c["z"].wait_recv()
        dx_ref[pl.ds(low, size)] = dxs[n][core, y, pl.ds(zl * size, size)] + dz[n][...]
        yield

    early = first_slot[-1]
    parts = {
        "g": row_gather(g_all),
        "x": row_gather(x_all),
        "p": col_gather(p_block(p_main, slots, cross), slots - cross),
        "q": col_gather(p_block(p_main, slots, 0), cross, z_first=False),
        "tab": tables(),
        "wo": w_out_split(),
        "wi": w_in_split(),
        "pack": pack_g(),
        "own": own_rows(),
        "gt": transposed(g_all, gt_hi, gt_lo, True),
        "xt": transposed(x_all, xt_hi, xt_lo, False),
        "dwo": w_out_grad(),
        "dwf": w_out_last(),
        "t0": row_sum(0, 0, early),
        "t1": row_sum(1, early, OWN),
    }
    if spare:
        parts["o"] = col_gather(p_block(p_over, spare, 0), spare)
    for j in range(len(chunks)):
        parts[f"s{j}"] = col_sum(j)
        parts[f"a{j}"] = col_gather(pg_block(j), chunks[j] * TILE)
        parts[f"dx{j}"] = x_grad(j)
        parts[f"dw{j}"] = w_in_grad(j)
    for name in ORDER:
        if name in parts:
            next(parts[name])
    for left in parts.values():
        assert next(left, None) is None
    for copy in started:
        copy.wait_send()
    assert len(started) <= COPIES


def grad_kernel(slots, out_grad, inputs, pre_act, w_in, w_out, kept):
    chunks, cross = PLANS[slots]
    spare = OWN - slots
    early = slots - chunks[-1]
    vmem = pl.BlockSpec(memory_space=pltpu.VMEM)
    anywhere = pl.BlockSpec(memory_space=pl.ANY)

    def room(*shape, dtype=F32):
        return pltpu.VMEM(shape, dtype)

    half = functools.partial(room, dtype=BF16)

    def each(make):
        return [make(t * TILE) for t in chunks]

    def both(make):
        return [make(early), make(OWN - early)]

    dx, dwin, dwout = pl.pallas_call(
        functools.partial(kernel, slots, chunks, cross),
        out_shape=(
            jax.ShapeDtypeStruct((OWN, TILE, D), F32),
            jax.ShapeDtypeStruct((D, F), F32),
            jax.ShapeDtypeStruct((F, D), F32),
        ),
        in_specs=[pl.BlockSpec(memory_space=pltpu.SMEM), vmem, vmem, vmem, anywhere, anywhere],
        out_specs=(vmem, vmem, vmem),
        scratch_shapes=[
            pltpu.SMEM((HALVES * slots,), jnp.int32),
            pltpu.SMEM((TILES,), jnp.int32),
            room(TILES, TILE, D),
            room(TILES, TILE, D),
            room(HALVES * slots, TILE, F),
            room(max(HALVES * spare, 1), TILE, F),
            each(lambda r: room(HALVES, r, F)),
            each(lambda r: room(2, 2, r, F)),
            each(lambda r: room(2, 4, r, F)),
            each(lambda r: room(2, r - r // 16 * TILE, F)),
            each(lambda r: room(2, r, F)),
            each(lambda r: room(HALVES * r, F)),
            half(HALVES * slots * TILE, D),
            half(HALVES * slots * TILE, D),
            half(slots // 2, D, PAD),
            half(slots // 2, D, PAD),
            half(slots // 2, D, PAD),
            half(slots // 2, D, PAD),
            room(D, F),
            room(F, D),
            half(LANES, LC, D),
            half(LANES, LC, D),
            half(LANES, D, LC),
            half(LANES, D, LC),
            room(HALVES * slots, TILE, D),
            both(lambda e: room(2, 4, 2 * e, TILE, D)),
            both(lambda e: room(4, 2 * e, TILE, D)),
            both(lambda e: room(2, e, TILE, D)),
            both(lambda e: room(2, 2 * e, TILE, D)),
            both(lambda e: room(e, TILE, D)),
            room(LANES, D, LC),
            room(SAMPLE_TILES, TILE, D),
            room(PAD, F),
            each(lambda r: room(r, F)),
            pltpu.SMEM((4, HALVES), jnp.int32),
            pltpu.SemaphoreType.DMA((COPIES,)),
            pltpu.SemaphoreType.DMA((COPIES,)),
            pltpu.SemaphoreType.DMA((2,)),
        ],
        compiler_params=pltpu.CompilerParams(
            collective_id=slots, has_side_effects=True, vmem_limit_bytes=64 * 1024 * 1024
        ),
        cost_estimate=pl.CostEstimate(flops=24 * slots * ROWS * D * F, bytes_accessed=6 * 1024 * 1024, transcendentals=0),
    )(
        kept,
        out_grad.reshape(OWN, TILE, D),
        inputs.reshape(OWN, TILE, D),
        pre_act.reshape(OWN, TILE, F),
        w_in,
        w_out,
    )
    return dx.reshape(ROWS, D), dwin, dwout


def settle_kernel(*refs):
    sources, targets, rooms, sems = refs[:3], refs[3:6], refs[6:9], refs[9]
    pieces = []
    for source, target, space in zip(sources, targets, rooms):
        rows = source.shape[0] // 2
        pieces += [
            tuple(ref.at[pl.ds(k * rows, rows)] for ref in (source, space, target)) for k in range(2)
        ]
    inward = [
        pltpu.make_async_copy(a, b, sems.at[0, k]) for k, (a, b, _) in enumerate(pieces)
    ]
    outward = [
        pltpu.make_async_copy(b, c, sems.at[1, k]) for k, (_, b, c) in enumerate(pieces)
    ]
    for copy in inward:
        copy.start()
    for first, second in zip(inward, outward):
        first.wait()
        second.start()
    for copy in outward:
        copy.wait()


def settle(*arrays):
    anywhere = pl.BlockSpec(memory_space=pl.ANY)
    return pl.pallas_call(
        settle_kernel,
        out_shape=tuple(jax.ShapeDtypeStruct(a.shape, a.dtype) for a in arrays),
        in_specs=[anywhere] * 3,
        out_specs=(anywhere,) * 3,
        scratch_shapes=[pltpu.VMEM(a.shape, a.dtype) for a in arrays]
        + [pltpu.SemaphoreType.DMA((2, 6))],
        compiler_params=pltpu.CompilerParams(vmem_limit_bytes=60 * 1024 * 1024),
    )(*arrays)


def shards(*args):
    tiles = jnp.sum((args[-1] + (TILE - 1)) // TILE)
    choices = sorted(PLANS)
    index = sum((tiles > HALVES * slots).astype(jnp.int32) for slots in choices[:-1])
    grads = lax.switch(index, [functools.partial(grad_kernel, slots) for slots in choices], *args)
    return settle(*grads)


def solution(mesh):
    return jax.shard_map(
        shards,
        mesh=mesh,
        in_specs=(
            P("row", "col"),
            P("row", "col"),
            P("col", "row"),
            P("col", "row"),
            P("row", "col"),
            P(),
        ),
        out_specs=(P("row", "col"), P("col", "row"), P("row", "col")),
        check_vma=False,
    )
```

time: 177 us -> 163 us (0.921)
  Pallas kernels: 167 us -> 158 us
  local copies, waits for them, and re-layouts: 5.09 us -> 0 us
    pallas_call x1 -> x2, Pallas kernels: 167 us -> 158 us  [the longest x1 155 us: grad_kernel(): pl.pallas_call(functools.partial(kernel, slots, chunks, cross), out_shape...]
    unnamed x5 -> x0, local copies, waits for them, and re-layouts: 5.09 us -> none
where the time goes in v3:
time: 163 us; the launch traced here: 162 us
  Pallas kernels  158 us (97%)
  between operations  2.12 us (1%)
    pallas_call x1, Pallas kernels, grad_kernel(): pl.pallas_call(functools.partial(kernel, slots, chunks, cross), out_shape...  155 us

profile of v3, /device:TPU:2, one launch (start us, length us, event | category | flops | bytes accessed | tf_op | source)
XLA Modules:
  0.0 161.9 jit_solution(16902363263372376159)
XLA Ops:
  0.6 1.3 fusion
  3.2 155.8 %conditional.1 = (f32[128,384]{1,0:T(8,128)}, f32[384,768]{1,0:T(8,128)}, f32[768,384]{1,0:T(8,128)}) conditional(s32[]{:T(128)} %clamp.3, (f32[128,384]{1,0:T(8,128)}, f32[128,384]{1,0:T(8,128)}, f32[128,768]{1,0:T(8,128)}, s32[8]{0:T(128)}, f32[384,768]{1,0:T(8,128)}, /*index=5*/f32[768,384]{1,0:T(8,128)}) %tuple.19, ...), branch_computations={%region_1.2_spmd, %region_2.3_spmd, %region_3.4_spmd} | conditional | flops 14495514624 | bytes 6291480 | solution.py:734
  3.5 155.0 %branch_1_fun.1 = (f32[16,8,384]{2,1,0:T(8,128)}, f32[384,768]{1,0:T(8,128)}, f32[768,384]{1,0:T(8,128)}) custom-call(s32[8]{0:T(128)} %get-tuple-element.45.kept_ref, f32[16,8,384]{2,1,0:T(8,128)} %bitcast.19, f32[16,8,384]{2,1,0:T(8,128)} %bitcast.22, f32[16,8,768]{2,1,0:T(8,128)} %bitcast.16, f32[384,768]{1,0:T(8,128)} %get-tuple-element.49.win_hbm, ...), custom_call_target="tpu_custom_call" | custom-call | flops 10871635968 | bytes 6291456 | tf_op jit(solution)/shard_map/cond/branch_1_fun/pallas_call | solution.py:630
  159.0 2.7 %shard_map.85 = (f32[128,384]{1,0:T(8,128)}, f32[384,768]{1,0:T(8,128)}, f32[768,384]{1,0:T(8,128)}) custom-call(f32[128,384]{1,0:T(8,128)} %get-tuple-element.69.refs_0_, f32[384,768]{1,0:T(8,128)} %get-tuple-element.70.refs_1_, f32[768,384]{1,0:T(8,128)} %get-tuple-element.71.refs_2_), custom_call_target="tpu_custom_call" | custom-call | tf_op jit(solution)/shard_map/pallas_call | solution.py:719

commit v4 on v3

--- a/solution.py
+++ b/solution.py
@@ -29,6 +29,15 @@
     "a0", "dx0", "a2", "a1", "dx1", "a2", "t0", "t0", "a2", "x", "x", "t0", "x", "a2", "t0", "t0", "t0", "t0",
     "a2", "dx2", "t1", "t1", "t0", "x", "t1", "t1", "t1", "t1", "x", "xt", "t1", "t0", "t1", "xt", "dw0", "t0",
     "t1", "dw1", "dw2", "t1",
+)
+ORDER_FULL = (
+    "p", "g", "tab", "tab", "tab", "tab", "wo", "own", "q", "p", "g", "g", "g", "p", "p", "g", "g", "g", "g",
+    "q", "q", "q", "g", "pack", "s0", "p", "p", "p", "wi", "gt", "q", "gt", "q", "s0", "s0", "s1", "x", "p", "q",
+    "q", "s0", "s1", "s1", "s2", "q", "s0", "s0", "p", "dwo", "s0", "a0", "s1", "s2", "dwo", "s2", "dwo", "a0",
+    "a0", "a0", "dwf", "s1", "s1", "s2", "a0", "a0", "x", "x", "x", "a0", "s1", "a1", "s2", "s2", "a0", "x", "x",
+    "x", "a1", "x", "a1", "a1", "x", "xt", "a0", "s2", "a2", "dx0", "a1", "a1", "xt", "a1", "dw0", "a1", "a2",
+    "a2", "a2", "a2", "a1", "dx1", "t0", "t0", "a2", "a2", "dw1", "t0", "t0", "t0", "a2", "t0", "a2", "dx2",
+    "t0", "t0", "t1", "t1", "dw2", "t1", "t1", "t1", "t1", "t0", "t1", "t1", "t1", "t0", "t1",
 )
 PLANS = {10: ((4, 4, 2), 5), 12: ((4, 4, 4), 6), 16: ((6, 6, 4), 8)}
 LC = 256
@@ -599,9 +608,8 @@
         parts[f"a{j}"] = col_gather(pg_block(j), chunks[j] * TILE)
         parts[f"dx{j}"] = x_grad(j)
         parts[f"dw{j}"] = w_in_grad(j)
-    for name in ORDER:
-        if name in parts:
-            next(parts[name])
+    for name in ORDER if spare else ORDER_FULL:
+        next(parts[name])
     for left in parts.values():
         assert next(left, None) is None
     for copy in started:

time: 163 us -> 163 us (level)
  no operation moved by 1% of the time
where the time goes in v4:
time: 163 us; the launch traced here: 162 us
  Pallas kernels  158 us (97%)
  between operations  2.12 us (1%)
    pallas_call x1, Pallas kernels, grad_kernel(): pl.pallas_call(functools.partial(kernel, slots, chunks, cross), out_shape...  155 us

profile of v4, /device:TPU:2, one launch (start us, length us, event | category | flops | bytes accessed | tf_op | source)
XLA Modules:
  0.0 161.9 jit_solution(8004781491273616025)
XLA Ops:
  0.6 1.3 fusion
  3.2 155.8 %conditional.1 = (f32[128,384]{1,0:T(8,128)}, f32[384,768]{1,0:T(8,128)}, f32[768,384]{1,0:T(8,128)}) conditional(s32[]{:T(128)} %clamp.3, (f32[128,384]{1,0:T(8,128)}, f32[128,384]{1,0:T(8,128)}, f32[128,768]{1,0:T(8,128)}, s32[8]{0:T(128)}, f32[384,768]{1,0:T(8,128)}, /*index=5*/f32[768,384]{1,0:T(8,128)}) %tuple.19, ...), branch_computations={%region_1.2_spmd, %region_2.3_spmd, %region_3.4_spmd} | conditional | flops 14495514624 | bytes 6291480 | solution.py:742
  3.5 155.0 %branch_1_fun.1 = (f32[16,8,384]{2,1,0:T(8,128)}, f32[384,768]{1,0:T(8,128)}, f32[768,384]{1,0:T(8,128)}) custom-call(s32[8]{0:T(128)} %get-tuple-element.45.kept_ref, f32[16,8,384]{2,1,0:T(8,128)} %bitcast.19, f32[16,8,384]{2,1,0:T(8,128)} %bitcast.22, f32[16,8,768]{2,1,0:T(8,128)} %bitcast.16, f32[384,768]{1,0:T(8,128)} %get-tuple-element.49.win_hbm, ...), custom_call_target="tpu_custom_call" | custom-call | flops 10871635968 | bytes 6291456 | tf_op jit(solution)/shard_map/cond/branch_1_fun/pallas_call | solution.py:638
  159.0 2.7 %shard_map.85 = (f32[128,384]{1,0:T(8,128)}, f32[384,768]{1,0:T(8,128)}, f32[768,384]{1,0:T(8,128)}) custom-call(f32[128,384]{1,0:T(8,128)} %get-tuple-element.69.refs_0_, f32[384,768]{1,0:T(8,128)} %get-tuple-element.70.refs_1_, f32[768,384]{1,0:T(8,128)} %get-tuple-element.71.refs_2_), custom_call_target="tpu_custom_call" | custom-call | tf_op jit(solution)/shard_map/pallas_call | solution.py:727
